TPU v7x, 256 devices: a whole 4x4x8 slice. The times are simulated.
256 devices in a mesh: row: 8 (over z), col: 16 (over x, y), vox: 2 (over core).
Axes of the slice: x: 4, y: 4, z: 8, core: 2. Of those that a mesh axis runs over, the one named last changes fastest.
Arguments:
- maps: bfloat16 [16384, 2048], P(('row', 'col'), 'vox'), may hold values from -21 to 21
- probes: bfloat16 [16384, 256], P(('row', 'col')), may hold values from -0.046875 to 0.046875
Outputs:
- gram: float32 [16384, 8, 16, 128], P('row', 'vox', 'col')
- basis: float32 [16384, 256], P(('row', 'col', 'vox'))
- factor: float32 [256, 256], replicated
All inputs are finite; a program needn't handle non-finite values.
Results may differ from a plain program's by a relative error of at most 0.004.
Values may be sent and summed in bfloat16 or wider, within the bound.
No kernel may reach another device: no remote copies, remote signals or barrier semaphores. Data moves between devices by JAX's collectives and lax.ppermute only.
A program may use at most 64 MiB of HBM per device.

v0:
```python
import jax
import jax.numpy as jnp
from jax import lax
from jax.sharding import PartitionSpec as P

VOX = 2048


def block_product(piece, partner):
    return (
        lax.dot_general(
            piece, partner, (((1,), (1,)), ((), ())), preferred_element_type=jnp.float32
        )
        / VOX
    )


def shards(maps, probes):
    sub_rows = maps.shape[0]
    row_count = lax.axis_size("row")
    col_count = lax.axis_size("col")
    vox_count = lax.axis_size("vox")
    subjects = sub_rows * row_count * col_count
    half_groups = row_count // vox_count
    vox_pos = lax.axis_index("vox")
    flat = maps.astype(jnp.float32)
    totals = lax.psum(jnp.sum(flat, axis=0), ("row", "col"))
    centered = (flat - totals[None, :] / subjects).astype(jnp.bfloat16)
    own_start = vox_pos * half_groups * sub_rows
    own_count = half_groups * sub_rows
    partial_sketch = None
    col_maps, col_probes = (
        lax.all_gather(centered, "row", axis=0, tiled=True),
        lax.all_gather(probes, "row", axis=0, tiled=True),
    )
    tile = block_product(lax.all_gather(centered, "col", axis=0, tiled=True), col_maps)
    block_rows = tile.shape[0]
    gram = lax.psum_scatter(
        tile.reshape(block_rows, row_count, 1, sub_rows), "vox", scatter_dimension=1, tiled=True
    )
    own_probes = lax.dynamic_slice_in_dim(col_probes, own_start, own_count, 0)
    partial_sketch = jnp.dot(
        gram.reshape(block_rows, own_count),
        own_probes.astype(jnp.float32),
        precision=lax.Precision.HIGHEST,
    )
    sketch = lax.psum_scatter(partial_sketch, ("col", "vox"), scatter_dimension=0, tiled=True)
    local_cross = lax.dot_general(
        sketch, sketch, (((0,), (0,)), ((), ())), precision=lax.Precision.HIGHEST
    )
    cross = lax.psum(local_cross, ("row", "col", "vox")) / subjects
    lower = jnp.linalg.cholesky(cross)
    basis = jax.scipy.linalg.solve_triangular(lower, sketch.T, lower=True).T
    return (gram, basis, lower.T)


def solution(mesh):
    placed = (P(("row", "col"), "vox"), P(("row", "col"), None))
    return jax.shard_map(
        shards,
        mesh=mesh,
        in_specs=placed,
        out_specs=(P("row", "vox", "col", None), P(("row", "col", "vox"), None), P()),
        check_vma=False,
    )
```

profile of v0, /device:TPU:2, one launch (start us, length us, event | category | flops | bytes accessed | tf_op | source)
XLA Modules:
  0.0 926.2 jit_solution(6317984655225748700)
XLA Ops:
  7.2 1.0 convert_reduce_fusion
  8.2 342.4 %psum.14 = f32[1024]{0:T(1024)S(1)} all-reduce(f32[1024]{0:T(1024)S(1)} %convert_reduce_fusion), channel_id=1, replica_groups=mesh['row'=8,'col'=16,'vox'=2] {'row','col'}, use_global_device_ids=true, to_apply=%region_1.0 | all-reduce | flops 1024 | bytes 8192 | tf_op jit(solution)/shard_map/psum | solution.py:27
  350.6 1.7 fusion
  352.4 0.7 all-gather.3.cloned.1.call-update
  353.1 42.8 %all-gather.5.cloned.1.call-done = bf16[1024,1024]{1,0:T(8,128)(2,1)} async-done(((bf16[128,1024]{1,0:T(8,128)(2,1)}), bf16[1024,1024]{1,0:T(8,128)(2,1)}) %all-gather.5.cloned.1.call-update) | async-done | bytes 2097168 | tf_op jit(solution)/shard_map/all_gather | solution.py:33
  396.0 58.1 %all-gather.3.cloned.1.call-done = bf16[2048,1024]{1,0:T(8,128)(2,1)} async-done(((bf16[128,1024]{1,0:T(8,128)(2,1)}), bf16[2048,1024]{1,0:T(8,128)(2,1)}) %all-gather.3.cloned.1.call-update) | async-done | bytes 4194320 | tf_op jit(solution)/shard_map/all_gather | solution.py:36
  454.1 10.6 %convolution_multiply_fusion = f32[2048,1024]{0,1:T(8,128)} fusion(bf16[2048,1024]{1,0:T(8,128)(2,1)} %all-gather.3.cloned.1.call-done, bf16[1024,1024]{1,0:T(8,128)(2,1)} %all-gather.5.cloned.1.call-done), kind=kOutput, calls=%fused_computation.2 | convolution fusion | flops 4297064448 | bytes 14680064 | tf_op jit(solution)/shard_map/dot_general | solution.py:11
  464.7 9.1 copy.14
  473.9 0.8 copy-done.1
  474.7 26.8 %all_gather.11 = bf16[1024,256]{1,0:T(8,128)(2,1)S(1)} all-gather(bf16[128,256]{1,0:T(8,128)(2,1)S(1)} %copy-done.1), channel_id=1, replica_groups=mesh['row'=8,'col'=16,'vox'=2] {'row'}, dimensions={0}, use_global_device_ids=true | all-gather | bytes 589824 | tf_op jit(solution)/shard_map/all_gather | solution.py:34
  501.4 5.3 copy.15
  506.8 7.0 fusion.2
  514.0 84.6 %reduce-scatter.5.cloned.1.call-done = f32[64,256]{1,0:T(8,128)} async-done(((f32[2048,256]{1,0:T(8,128)}), f32[64,256]{1,0:T(8,128)}) %reduce-scatter.5.cloned.1.call-update) | async-done | bytes 65552 | tf_op jit(solution)/shard_map/reduce_scatter | solution.py:47
  598.6 2.0 fusion.15
  600.6 8.4 copy.18
  609.1 246.4 %all-reduce.3.cloned.1.call-done = f32[256,256]{0,1:T(8,128)} async-done(((f32[256,256]{0,1:T(8,128)}), f32[256,256]{0,1:T(8,128)}) %all-reduce.3.cloned.1.call-update) | async-done | bytes 262160 | tf_op jit(solution)/shard_map/psum | solution.py:51
  855.5 1.0 broadcast_multiply_fusion
  856.6 1.0 fusion.1
  857.6 11.7 %cholesky.50 = f32[128,128]{1,0:T(8,128)S(1)} custom-call(f32[128,128]{1,0:T(8,128)S(1)} %cholesky.118), custom_call_target="Cholesky" | custom-call | tf_op jit(solution)/shard_map/jit(cholesky)/cholesky | solution.py:52
  869.3 9.8 %custom-call.15 = f32[1,128,128]{1,2,0:T(8,128)S(1)} custom-call(f32[1,128,128]{2,1,0:T(8,128)S(1)} %get-tuple-element.35), custom_call_target="InvertDiagBlocksLowerTriangular" | custom-call | tf_op jit(solution)/shard_map/jit(cholesky)/cholesky | solution.py:52
  879.4 0.3 convolution_subtract_fusion
  879.6 11.7 %cholesky.105 = f32[128,128]{1,0:T(8,128)S(1)} custom-call(f32[128,128]{1,0:T(8,128)S(1)} %convolution_subtract_fusion), custom_call_target="Cholesky" | custom-call | tf_op jit(solution)/shard_map/jit(cholesky)/cholesky | solution.py:52
  891.4 0.7 compare_reduce_fusion
  893.6 4.1 while.1
  893.6 0.6 fusion.26
  894.2 1.4 bitcast_dynamic-update-slice_fusion.2
  895.6 0.6 fusion.26
  896.2 1.4 bitcast_dynamic-update-slice_fusion.2
  897.7 19.9 %custom-call.16 = f32[2,128,128]{1,2,0:T(8,128)S(1)} custom-call(f32[2,128,128]{2,1,0:T(8,128)S(1)} %get-tuple-element.10), custom_call_target="InvertDiagBlocksLowerTriangular" | custom-call | tf_op jit(solution)/shard_map/jit(_solve_triangular)/triangular_solve | solution.py:53
  917.8 0.2 convolution_subtract_fusion.1
  918.2 0.6 maximum_bitcast_fusion
  918.8 0.8 copy.19
  (28 shorter events, 1.4 us)
Async XLA Ops:
  7.2 388.8 %all-gather.5.cloned.1.call-start = ((), (), s32[]{:S(2)}) async-start(), calls=%async_computation.3 | async-start | bytes 2359296 | tf_op jit(solution)/shard_map/all_gather | solution.py:33
  352.3 101.7 %all-gather.3.cloned.1.call-start = ((), (), s32[]{:S(2)}) async-start(), calls=%async_computation.2 | async-start | bytes 4456448 | tf_op jit(solution)/shard_map/all_gather | solution.py:36
  353.1 148.3 %reduce-scatter.3.cloned.1.call-start = ((), (), s32[]{:S(2)}) async-start(), calls=%async_computation.4 | async-start | bytes 12582912 | tf_op jit(solution)/shard_map/reduce_scatter | solution.py:38
  473.8 0.8 copy-start.1
  473.9 124.7 %reduce-scatter.5.cloned.1.call-start = ((), (), s32[]{:S(2)}) async-start(), calls=%async_computation.5 | async-start | bytes 2162688 | tf_op jit(solution)/shard_map/reduce_scatter | solution.py:47
  513.8 341.7 %all-reduce.3.cloned.1.call-start = ((), (), s32[]{:S(2)}) async-start(), calls=%async_computation.6 | async-start | bytes 524288 | tf_op jit(solution)/shard_map/psum | solution.py:51
  609.1 308.5 %copy-start = (f32[64,256]{1,0:T(8,128)S(1)}, f32[64,256]{1,0:T(8,128)}, u32[]{:S(2)}) copy-start(f32[64,256]{1,0:T(8,128)} %reduce-scatter.5.cloned.1.call-done) | copy-start | bytes 196612
Sparse Core Ops, SparseCore 0:
  352.5 43.4 all-gather.4
  399.0 55.0 all-gather.2
  474.0 21.9 reduce-scatter.2
  513.9 84.6 reduce-scatter.4
  605.3 250.0 all-reduce.2
where the time goes:
time: 927 us; the launch traced here: 926 us
  waiting for transfers between devices  433 us (47%)
  blocking collectives  369 us (40%)
  other arithmetic  59.3 us (6%)
  local copies, waits for them, and re-layouts  28.8 us (3%)
  matrix products  20.7 us (2%)
  between operations  15.2 us (2%)
    psum x1, blocking collectives, shards(): totals = lax.psum(jnp.sum(flat, axis=0), ('row', 'col'))  342 us
    psum x1, waiting for transfers between devices, shards(): cross = lax.psum(local_cross, ('row', 'col', 'vox')) / subjects  246 us
    reduce_scatter x1, waiting for transfers between devices, shards(): lax.psum_scatter(partial_sketch, ('col', 'vox'), scatter_dimension=0, til...  84.6 us
    all_gather x1, waiting for transfers between devices, shards(): lax.all_gather(centered, 'col', axis=0, tiled=True)  58.1 us
    all_gather x1, waiting for transfers between devices, shards(): lax.all_gather(centered, 'row', axis=0, tiled=True)  42.8 us
    another operation x6, other arithmetic, shards(): lower = jnp.linalg.cholesky(cross)  34 us
    all_gather x1, blocking collectives, shards(): lax.all_gather(probes, 'row', axis=0, tiled=True)  26.8 us
    another operation x2, other arithmetic, shards(): basis = jax.scipy.linalg.solve_triangular(lower, sketch.T, lower=True).T  19.9 us
  transfers between devices with their start and end apart: 5, of which 4 were waited for; matrix products, arithmetic and copies ran while one was open for 1% of the time, Pallas kernels for 0%

commit v1 on v0

--- a/solution.py
+++ b/solution.py
@@ -1,9 +1,24 @@
+import functools
 import jax
 import jax.numpy as jnp
 from jax import lax
 from jax.sharding import PartitionSpec as P
 
 VOX = 2048
+
+
+def detail_the_series_all(incoming_x, ndim_at):
+    n_parts = lax.axis_size("col")
+    vals = []
+    for to_i in range(incoming_x.ndim):
+        vals.append(n_parts if to_i == ndim_at else 1)
+    m_next = lax.all_to_all(
+        jnp.tile(incoming_x, vals), "col", split_axis=ndim_at, concat_axis=ndim_at, tiled=True
+    )
+    return m_next
+
+
+_fix_kinds = functools.partial(detail_the_series_all, ndim_at=0)
 
 
 def block_product(piece, partner):
@@ -33,7 +48,7 @@
         lax.all_gather(centered, "row", axis=0, tiled=True),
         lax.all_gather(probes, "row", axis=0, tiled=True),
     )
-    tile = block_product(lax.all_gather(centered, "col", axis=0, tiled=True), col_maps)
+    tile = block_product(_fix_kinds(centered), col_maps)
     block_rows = tile.shape[0]
     gram = lax.psum_scatter(
         tile.reshape(block_rows, row_count, 1, sub_rows), "vox", scatter_dimension=1, tiled=True

time: 927 us -> 888 us (0.958)
  waiting for transfers between devices: 433 us -> 372 us
  starting transfers between devices: 0.38 us -> 15.5 us
    all_gather x1 -> x0, waiting for transfers between devices: 58.1 us -> none  [shards(): lax.all_gather(centered, 'col', axis=0, tiled=True)]
    all_to_all x0 -> x1, starting transfers between devices: none -> 15.1 us  [detail_the_series_all(): lax.all_to_all(jnp.tile(incoming_x, vals), 'col', split_axis=ndim_at, con...]
  transfers between devices with their start and end apart: 5 -> 5, of which waited for: 4 -> 3; matrix products, arithmetic and copies ran while one was open for 1% -> 1% of each run, Pallas kernels for 0% -> 0%
where the time goes in v1:
time: 888 us; the launch traced here: 887 us
  blocking collectives  373 us (42%)
  waiting for transfers between devices  372 us (42%)
  other arithmetic  58.6 us (7%)
  local copies, waits for them, and re-layouts  31.3 us (4%)
  matrix products  20.7 us (2%)
  starting transfers between devices  15.5 us (2%)
  between operations  15.3 us (2%)
    psum x1, blocking collectives, shards(): totals = lax.psum(jnp.sum(flat, axis=0), ('row', 'col'))  348 us
    psum x1, waiting for transfers between devices, shards(): cross = lax.psum(local_cross, ('row', 'col', 'vox')) / subjects  246 us
    reduce_scatter x1, waiting for transfers between devices, shards(): lax.psum_scatter(partial_sketch, ('col', 'vox'), scatter_dimension=0, til...  84.6 us
    all_gather x1, waiting for transfers between devices, shards(): lax.all_gather(centered, 'row', axis=0, tiled=True)  40.5 us
    another operation x6, other arithmetic, shards(): lower = jnp.linalg.cholesky(cross)  34 us
    all_gather x1, blocking collectives, shards(): lax.all_gather(probes, 'row', axis=0, tiled=True)  25.5 us
    another operation x2, other arithmetic, shards(): basis = jax.scipy.linalg.solve_triangular(lower, sketch.T, lower=True).T  19.9 us
  transfers between devices with their start and end apart: 5, of which 3 were waited for; matrix products, arithmetic and copies ran while one was open for 1% of the time, Pallas kernels for 0%

profile of v1, /device:TPU:2, one launch (start us, length us, event | category | flops | bytes accessed | tf_op | source)
XLA Modules:
  0.0 886.8 jit_solution(3717286401033120403)
XLA Ops:
  7.2 1.0 convert_reduce_fusion
  8.2 347.7 %psum.14 = f32[1024]{0:T(1024)S(1)} all-reduce(f32[1024]{0:T(1024)S(1)} %convert_reduce_fusion), channel_id=1, replica_groups=mesh['row'=8,'col'=16,'vox'=2] {'row','col'}, use_global_device_ids=true, to_apply=%region_1.0 | all-reduce | flops 1024 | bytes 8192 | tf_op jit(solution)/shard_map/psum | solution.py:42
  355.9 1.0 fusion
  356.9 2.5 tile.2
  359.5 15.1 %all-to-all-start = ((bf16[16,128,1024]{2,1,0:T(8,128)(2,1)}), bf16[16,128,1024]{2,1,0:T(8,128)(2,1)}, u32[]{:S(2)}, u32[]{:S(2)}) async-start(bf16[16,128,1024]{2,1,0:T(8,128)(2,1)} %tile.2), calls=%async_computation | async-start | bytes 8388608 | tf_op jit(solution)/shard_map/all_to_all | solution.py:15
  374.6 0.7 all-gather.2.cloned.1.call-update
  375.4 40.5 %all-gather.2.cloned.1.call-done = bf16[1024,1024]{1,0:T(8,128)(2,1)} async-done(((bf16[128,1024]{1,0:T(8,128)(2,1)}), bf16[1024,1024]{1,0:T(8,128)(2,1)}) %all-gather.2.cloned.1.call-update) | async-done | bytes 2097168 | tf_op jit(solution)/shard_map/all_gather | solution.py:48
  415.9 10.6 %convolution_multiply_fusion = f32[2048,1024]{0,1:T(8,128)} fusion(bf16[2048,1024]{1,0:T(8,128)(2,1)} %bitcast, bf16[1024,1024]{1,0:T(8,128)(2,1)} %all-gather.2.cloned.1.call-done), kind=kOutput, calls=%fused_computation.2 | convolution fusion | flops 4297064448 | bytes 14680064 | tf_op jit(solution)/shard_map/dot_general | solution.py:26
  426.6 9.1 %copy.14 = f32[2048,8,1,128]{3,0,2,1:T(8,128)} copy(f32[2048,8,1,128]{0,3,1,2:T(8,128)} %bitcast.45) | data formatting | bytes 16777216 | tf_op jit(solution)/shard_map/reshape | solution.py:54
  435.8 0.8 copy-done.2
  436.5 25.5 %all_gather.7 = bf16[1024,256]{1,0:T(8,128)(2,1)S(1)} all-gather(bf16[128,256]{1,0:T(8,128)(2,1)S(1)} %copy-done.2), channel_id=1, replica_groups=mesh['row'=8,'col'=16,'vox'=2] {'row'}, dimensions={0}, use_global_device_ids=true | all-gather | bytes 589824 | tf_op jit(solution)/shard_map/all_gather | solution.py:49
  462.0 5.3 copy.15
  467.4 7.0 fusion.2
  474.6 84.6 %reduce-scatter.5.cloned.1.call-done = f32[64,256]{1,0:T(8,128)} async-done(((f32[2048,256]{1,0:T(8,128)}), f32[64,256]{1,0:T(8,128)}) %reduce-scatter.5.cloned.1.call-update) | async-done | bytes 65552 | tf_op jit(solution)/shard_map/reduce_scatter | solution.py:62
  559.2 2.0 fusion.15
  561.3 8.4 copy.18
  569.7 246.3 %all-reduce.3.cloned.1.call-done = f32[256,256]{0,1:T(8,128)} async-done(((f32[256,256]{0,1:T(8,128)}), f32[256,256]{0,1:T(8,128)}) %all-reduce.3.cloned.1.call-update) | async-done | bytes 262160 | tf_op jit(solution)/shard_map/psum | solution.py:66
  816.0 1.0 broadcast_multiply_fusion
  817.1 1.0 fusion.1
  818.1 11.7 %cholesky.50 = f32[128,128]{1,0:T(8,128)S(1)} custom-call(f32[128,128]{1,0:T(8,128)S(1)} %cholesky.118), custom_call_target="Cholesky" | custom-call | tf_op jit(solution)/shard_map/jit(cholesky)/cholesky | solution.py:67
  829.9 9.8 %custom-call.15 = f32[1,128,128]{1,2,0:T(8,128)S(1)} custom-call(f32[1,128,128]{2,1,0:T(8,128)S(1)} %get-tuple-element.35), custom_call_target="InvertDiagBlocksLowerTriangular" | custom-call | tf_op jit(solution)/shard_map/jit(cholesky)/cholesky | solution.py:67
  839.9 0.3 convolution_subtract_fusion
  840.2 11.7 %cholesky.105 = f32[128,128]{1,0:T(8,128)S(1)} custom-call(f32[128,128]{1,0:T(8,128)S(1)} %convolution_subtract_fusion), custom_call_target="Cholesky" | custom-call | tf_op jit(solution)/shard_map/jit(cholesky)/cholesky | solution.py:67
  851.9 0.7 compare_reduce_fusion
  854.1 4.1 while.1
  854.1 0.6 fusion.26
  854.7 1.4 bitcast_dynamic-update-slice_fusion.2
  856.2 0.6 fusion.26
  856.8 1.4 bitcast_dynamic-update-slice_fusion.2
  858.2 19.9 %custom-call.16 = f32[2,128,128]{1,2,0:T(8,128)S(1)} custom-call(f32[2,128,128]{2,1,0:T(8,128)S(1)} %get-tuple-element.10), custom_call_target="InvertDiagBlocksLowerTriangular" | custom-call | tf_op jit(solution)/shard_map/jit(_solve_triangular)/triangular_solve | solution.py:68
  878.8 0.6 maximum_bitcast_fusion
  879.4 0.8 copy.19
  (30 shorter events, 1.6 us)
Async XLA Ops:
  356.9 2.6 copy-start
  359.5 56.5 %all-to-all-start = ((bf16[16,128,1024]{2,1,0:T(8,128)(2,1)}), bf16[16,128,1024]{2,1,0:T(8,128)(2,1)}, u32[]{:S(2)}, u32[]{:S(2)}) async-start(bf16[16,128,1024]{2,1,0:T(8,128)(2,1)} %tile.2), calls=%async_computation | async-start | bytes 8388608 | tf_op jit(solution)/shard_map/all_to_all | solution.py:15
  374.6 41.3 %all-gather.2.cloned.1.call-start = ((), (), s32[]{:S(2)}) async-start(), calls=%async_computation.3 | async-start | bytes 2359296 | tf_op jit(solution)/shard_map/all_gather | solution.py:48
  375.3 86.7 %reduce-scatter.3.cloned.1.call-start = ((), (), s32[]{:S(2)}) async-start(), calls=%async_computation.4 | async-start | bytes 12582912 | tf_op jit(solution)/shard_map/reduce_scatter | solution.py:53
  435.7 0.8 copy-start.2
  435.7 123.5 %reduce-scatter.5.cloned.1.call-start = ((), (), s32[]{:S(2)}) async-start(), calls=%async_computation.5 | async-start | bytes 2162688 | tf_op jit(solution)/shard_map/reduce_scatter | solution.py:62
  474.3 341.7 %all-reduce.3.cloned.1.call-start = ((), (), s32[]{:S(2)}) async-start(), calls=%async_computation.6 | async-start | bytes 524288 | tf_op jit(solution)/shard_map/psum | solution.py:66
  569.7 308.4 %copy-start.1 = (f32[64,256]{1,0:T(8,128)S(1)}, f32[64,256]{1,0:T(8,128)}, u32[]{:S(2)}) copy-start(f32[64,256]{1,0:T(8,128)} %reduce-scatter.5.cloned.1.call-done) | copy-start | bytes 196612
Sparse Core Ops, SparseCore 0:
  377.8 38.0 all-gather.1
  435.8 20.8 reduce-scatter.2
  474.5 84.6 reduce-scatter.4
  566.0 250.0 all-reduce.2

commit v2 on v0

--- a/solution.py
+++ b/solution.py
@@ -24,7 +24,10 @@
     half_groups = row_count // vox_count
     vox_pos = lax.axis_index("vox")
     flat = maps.astype(jnp.float32)
-    totals = lax.psum(jnp.sum(flat, axis=0), ("row", "col"))
+    switch_signs_now = lambda values, chip_axis, peer_axis: lax.psum(
+        lax.psum(values, axis_name=chip_axis), axis_name=peer_axis
+    )
+    totals = switch_signs_now(jnp.sum(flat, axis=0), "row", "col")
     centered = (flat - totals[None, :] / subjects).astype(jnp.bfloat16)
     own_start = vox_pos * half_groups * sub_rows
     own_count = half_groups * sub_rows

time: 927 us -> 636 us (0.69)
  blocking collectives: 369 us -> 81.4 us
    psum x1 -> x2, blocking collectives: 342 us -> 54.6 us  [the longest x1 34.6 us: shards(): lax.psum(lax.psum(values, axis_name=chip_axis), axis_name=peer_axis)]
where the time goes in v2:
time: 636 us; the launch traced here: 635 us
  waiting for transfers between devices  429 us (67%)
  blocking collectives  81.4 us (13%)
  other arithmetic  59.3 us (9%)
  local copies, waits for them, and re-layouts  28.8 us (5%)
  matrix products  20.7 us (3%)
  between operations  15.2 us (2%)
    psum x1, waiting for transfers between devices, shards(): cross = lax.psum(local_cross, ('row', 'col', 'vox')) / subjects  246 us
    reduce_scatter x1, waiting for transfers between devices, shards(): lax.psum_scatter(partial_sketch, ('col', 'vox'), scatter_dimension=0, til...  84.6 us
    all_gather x1, waiting for transfers between devices, shards(): lax.all_gather(centered, 'col', axis=0, tiled=True)  58.1 us
    all_gather x1, waiting for transfers between devices, shards(): lax.all_gather(centered, 'row', axis=0, tiled=True)  39.6 us
    psum x1, blocking collectives, shards(): lax.psum(lax.psum(values, axis_name=chip_axis), axis_name=peer_axis)  34.6 us
    another operation x6, other arithmetic, shards(): lower = jnp.linalg.cholesky(cross)  34 us
    all_gather x1, blocking collectives, shards(): lax.all_gather(probes, 'row', axis=0, tiled=True)  26.8 us
    psum x1, blocking collectives, shards(): lax.psum(values, axis_name=chip_axis)  20 us
  transfers between devices with their start and end apart: 5, of which 4 were waited for; matrix products, arithmetic and copies ran while one was open for 1% of the time, Pallas kernels for 0%

profile of v2, /device:TPU:2, one launch (start us, length us, event | category | flops | bytes accessed | tf_op | source)
XLA Modules:
  0.0 635.2 jit_solution(14529822880203112052)
XLA Ops:
  7.2 1.0 convert_reduce_fusion
  8.2 20.0 %psum.21 = f32[1024]{0:T(1024)S(1)} all-reduce(f32[1024]{0:T(1024)S(1)} %convert_reduce_fusion), channel_id=1, replica_groups=mesh['row'=8,'col'=16,'vox'=2] {'row'}, use_global_device_ids=true, to_apply=%region_1.0 | all-reduce | flops 1024 | bytes 8192 | tf_op jit(solution)/shard_map/psum | solution.py:28
  28.2 34.6 %psum.22 = f32[1024]{0:T(1024)S(1)} all-reduce(f32[1024]{0:T(1024)S(1)} %psum.21), channel_id=1, replica_groups=mesh['row'=8,'col'=16,'vox'=2] {'col'}, use_global_device_ids=true, to_apply=%region_2.0 | all-reduce | flops 1024 | bytes 8192 | tf_op jit(solution)/shard_map/psum | solution.py:27
  62.8 1.7 fusion
  64.6 0.7 all-gather.3.cloned.1.call-update
  65.3 39.6 %all-gather.5.cloned.1.call-done = bf16[1024,1024]{1,0:T(8,128)(2,1)} async-done(((bf16[128,1024]{1,0:T(8,128)(2,1)}), bf16[1024,1024]{1,0:T(8,128)(2,1)}) %all-gather.5.cloned.1.call-update) | async-done | bytes 2097168 | tf_op jit(solution)/shard_map/all_gather | solution.py:36
  104.9 58.1 %all-gather.3.cloned.1.call-done = bf16[2048,1024]{1,0:T(8,128)(2,1)} async-done(((bf16[128,1024]{1,0:T(8,128)(2,1)}), bf16[2048,1024]{1,0:T(8,128)(2,1)}) %all-gather.3.cloned.1.call-update) | async-done | bytes 4194320 | tf_op jit(solution)/shard_map/all_gather | solution.py:39
  163.0 10.6 %convolution_multiply_fusion = f32[2048,1024]{0,1:T(8,128)} fusion(bf16[2048,1024]{1,0:T(8,128)(2,1)} %all-gather.3.cloned.1.call-done, bf16[1024,1024]{1,0:T(8,128)(2,1)} %all-gather.5.cloned.1.call-done), kind=kOutput, calls=%fused_computation.2 | convolution fusion | flops 4297064448 | bytes 14680064 | tf_op jit(solution)/shard_map/dot_general | solution.py:11
  173.7 9.1 %copy.14 = f32[2048,8,1,128]{3,0,2,1:T(8,128)} copy(f32[2048,8,1,128]{0,3,1,2:T(8,128)} %bitcast.44) | data formatting | bytes 16777216 | tf_op jit(solution)/shard_map/reshape | solution.py:42
  182.9 0.8 copy-done.1
  183.6 26.8 %all_gather.11 = bf16[1024,256]{1,0:T(8,128)(2,1)S(1)} all-gather(bf16[128,256]{1,0:T(8,128)(2,1)S(1)} %copy-done.1), channel_id=1, replica_groups=mesh['row'=8,'col'=16,'vox'=2] {'row'}, dimensions={0}, use_global_device_ids=true | all-gather | bytes 589824 | tf_op jit(solution)/shard_map/all_gather | solution.py:37
  210.4 5.3 copy.15
  215.7 7.0 %fusion.2 = f32[2048,256]{1,0:T(8,128)} fusion(f32[2048,512]{0,1:T(8,128)} %bitcast.43, bf16[1024,256]{1,0:T(8,128)(2,1)S(1)} %all_gather.11, s32[]{:T(128)S(6)} %select_n.7), kind=kOutput, calls=%fused_computation.11 | convolution fusion | flops 3221225472 | bytes 6553604 | tf_op jit(solution)/shard_map/dot_general | solution.py:45
  222.9 84.6 %reduce-scatter.5.cloned.1.call-done = f32[64,256]{1,0:T(8,128)} async-done(((f32[2048,256]{1,0:T(8,128)}), f32[64,256]{1,0:T(8,128)}) %reduce-scatter.5.cloned.1.call-update) | async-done | bytes 65552 | tf_op jit(solution)/shard_map/reduce_scatter | solution.py:50
  307.6 2.0 fusion.15
  309.6 8.4 %copy.18 = f32[2048,4,1,128]{3,2,1,0:T(1,128)} copy(f32[2048,4,1,128]{3,0,2,1:T(8,128)} %reduce-scatter.3.cloned.1.call-done) | data formatting | bytes 8388608
  318.1 246.3 %all-reduce.3.cloned.1.call-done = f32[256,256]{0,1:T(8,128)} async-done(((f32[256,256]{0,1:T(8,128)}), f32[256,256]{0,1:T(8,128)}) %all-reduce.3.cloned.1.call-update) | async-done | bytes 262160 | tf_op jit(solution)/shard_map/psum | solution.py:54
  564.4 1.0 broadcast_multiply_fusion
  565.5 1.0 fusion.1
  566.5 11.7 %cholesky.50 = f32[128,128]{1,0:T(8,128)S(1)} custom-call(f32[128,128]{1,0:T(8,128)S(1)} %cholesky.118), custom_call_target="Cholesky" | custom-call | tf_op jit(solution)/shard_map/jit(cholesky)/cholesky | solution.py:55
  578.3 9.8 %custom-call.15 = f32[1,128,128]{1,2,0:T(8,128)S(1)} custom-call(f32[1,128,128]{2,1,0:T(8,128)S(1)} %get-tuple-element.35), custom_call_target="InvertDiagBlocksLowerTriangular" | custom-call | tf_op jit(solution)/shard_map/jit(cholesky)/cholesky | solution.py:55
  588.3 0.3 convolution_subtract_fusion
  588.6 11.7 %cholesky.105 = f32[128,128]{1,0:T(8,128)S(1)} custom-call(f32[128,128]{1,0:T(8,128)S(1)} %convolution_subtract_fusion), custom_call_target="Cholesky" | custom-call | tf_op jit(solution)/shard_map/jit(cholesky)/cholesky | solution.py:55
  600.3 0.7 compare_reduce_fusion
  602.5 4.1 while.1
  602.5 0.6 fusion.26
  603.1 1.4 bitcast_dynamic-update-slice_fusion.2
  604.6 0.6 fusion.26
  605.2 1.4 bitcast_dynamic-update-slice_fusion.2
  606.6 19.9 %custom-call.16 = f32[2,128,128]{1,2,0:T(8,128)S(1)} custom-call(f32[2,128,128]{2,1,0:T(8,128)S(1)} %get-tuple-element.10), custom_call_target="InvertDiagBlocksLowerTriangular" | custom-call | tf_op jit(solution)/shard_map/jit(_solve_triangular)/triangular_solve | solution.py:56
  627.2 0.6 maximum_bitcast_fusion
  627.8 0.8 copy.19
  (29 shorter events, 1.6 us)
Async XLA Ops:
  7.2 97.7 %all-gather.5.cloned.1.call-start = ((), (), s32[]{:S(2)}) async-start(), calls=%async_computation.3 | async-start | bytes 2359296 | tf_op jit(solution)/shard_map/all_gather | solution.py:36
  64.5 98.5 %all-gather.3.cloned.1.call-start = ((), (), s32[]{:S(2)}) async-start(), calls=%async_computation.2 | async-start | bytes 4456448 | tf_op jit(solution)/shard_map/all_gather | solution.py:39
  65.3 145.1 %reduce-scatter.3.cloned.1.call-start = ((), (), s32[]{:S(2)}) async-start(), calls=%async_computation.4 | async-start | bytes 12582912 | tf_op jit(solution)/shard_map/reduce_scatter | solution.py:41
  182.8 0.8 copy-start.1
  182.8 124.8 %reduce-scatter.5.cloned.1.call-start = ((), (), s32[]{:S(2)}) async-start(), calls=%async_computation.5 | async-start | bytes 2162688 | tf_op jit(solution)/shard_map/reduce_scatter | solution.py:50
  222.7 341.7 %all-reduce.3.cloned.1.call-start = ((), (), s32[]{:S(2)}) async-start(), calls=%async_computation.6 | async-start | bytes 524288 | tf_op jit(solution)/shard_map/psum | solution.py:54
  318.1 308.5 %copy-start = (f32[64,256]{1,0:T(8,128)S(1)}, f32[64,256]{1,0:T(8,128)}, u32[]{:S(2)}) copy-start(f32[64,256]{1,0:T(8,128)} %reduce-scatter.5.cloned.1.call-done) | copy-start | bytes 196612
Sparse Core Ops, SparseCore 0:
  64.7 40.1 all-gather.4
  107.9 55.0 all-gather.2
  182.9 21.9 reduce-scatter.2
  222.8 84.6 reduce-scatter.4
  314.3 250.0 all-reduce.2
